TPU v7x, 256 devices: a whole 4x4x8 slice. The times are simulated.
256 devices in a mesh: blk: 16 (over x, y_lo, core), tm: 16 (over y_hi, z).
Axes of the slice: x: 4, y: 4 (y_hi: 2, y_lo: 2; y = y_hi * 2 + y_lo), z: 8, core: 2. Of those that a mesh axis runs over, the one named last changes fastest.
Arguments:
- readings: bfloat16 [65536, 16384], P('blk', 'tm'), may hold values from -6 to 6
- tile_mask: int32 [512, 128], P('blk', 'tm'), may hold values 0 or 1
- sensor_f: bfloat16 [65536, 256], P('blk'), may hold values from -6 to 6
- time_f: bfloat16 [16384, 256], P('tm'), may hold values from -6 to 6
- ar_weight: float32 [3, 256], replicated, may hold values from 0.1 to 0.45
Outputs:
- new_sensor_f: bfloat16 [65536, 256], P('blk')
- new_time_f: bfloat16 [16384, 256], P('tm')
All inputs are finite; a program needn't handle non-finite values. No bound on the sum of `tile_mask` on one device may be relied on, other than what follows from the above.
Results may differ from a plain program's by a relative error of at most 0.0041.
Values may be sent and summed in bfloat16 or wider, within the bound.
A program may use at most 128 MiB of HBM per device.

v0:
```python
import math

import jax
import jax.numpy as jnp
from jax import lax
from jax.sharding import PartitionSpec as P

TILE = 128
LAG = 96


def passed_along(block, axis, distance):
    devices = range(lax.axis_size(axis))
    route = [(i - distance, i) for i in devices if i - distance in devices]
    return lax.ppermute(block, axis, route)


def on_device(readings, tile_mask, sensor_f, time_f, ar_weight):
    rank_size = sensor_f.shape[1]
    scale = 1.0 / math.sqrt(rank_size)
    sens_here, time_here = readings.shape
    time_total = time_here * lax.axis_size("tm")
    sens_total = sens_here * lax.axis_size("blk")
    pred = jnp.dot(sensor_f, time_f.T, preferred_element_type=jnp.float32) * scale
    diff = (readings.astype(jnp.float32) - pred).reshape(
        sens_here // TILE, TILE, time_here // TILE, TILE
    )
    keep = tile_mask.astype(jnp.float32)[:, None, :, None]
    resid = (diff * keep).reshape(sens_here, time_here).astype(jnp.bfloat16)
    step_sens = 2.0 * math.sqrt(rank_size / time_total)
    step_time = 2.0 * math.sqrt(rank_size / sens_total)
    lags = (1, 12, LAG)
    grad_s = lax.psum(jnp.dot(resid, time_f, preferred_element_type=jnp.float32) * scale, "tm")
    new_sensor_f = (0.9 * sensor_f.astype(jnp.float32) + step_sens * grad_s).astype(jnp.bfloat16)
    lower_rim = passed_along(time_f[time_here - LAG :], "tm", 1)
    padded = jnp.concatenate([lower_rim, time_f], axis=0).astype(jnp.float32)
    ar_err = padded[LAG : LAG + time_here]
    for index in range(3):
        ar_err = (
            ar_err - ar_weight[index] * padded[LAG - lags[index] : LAG - lags[index] + time_here]
        )
    upper_rim = passed_along(ar_err[:LAG].astype(jnp.bfloat16), "tm", -1).astype(jnp.float32)
    err_pad = jnp.concatenate([ar_err, upper_rim], axis=0)
    ar_adj = ar_err
    for index in range(3):
        ar_adj = ar_adj - ar_weight[index] * err_pad[lags[index] : lags[index] + time_here]
    factor = time_f.astype(jnp.float32)
    grad_t = lax.psum(
        lax.dot_general(
            resid, sensor_f, (((0,), (0,)), ((), ())), preferred_element_type=jnp.float32
        )
        * scale,
        "blk",
    )
    new_time_f = (factor + step_time * grad_t - 0.5 * ar_adj).astype(jnp.bfloat16)
    return (new_sensor_f, new_time_f)


def solution(mesh):
    return jax.shard_map(
        on_device,
        mesh=mesh,
        in_specs=(P("blk", "tm"), P("blk", "tm"), P("blk", None), P("tm", None), P()),
        out_specs=(P("blk", None), P("tm", None)),
        check_vma=False,
    )
```

profile of v0, /device:TPU:2, one launch (start us, length us, event | category | flops | bytes accessed | tf_op | source)
XLA Modules:
  0.0 349.8 jit_solution(12207497294424615500)
XLA Ops:
  7.2 0.0 all-reduce.5.cloned.1.call-start
  7.2 0.7 convert_element_type.30
  7.9 0.1 copy.7
  8.0 0.0 copy-start.1
  8.0 0.0 copy-start.2
  8.0 6.9 %mul.105 = f32[32,128,8,128]{3,2,1,0:T(8,128)} broadcast(f32[32,8]{1,0:T(8,128)S(1)} %copy.7), dimensions={0,2} | broadcast | bytes 16778240 | tf_op jit(solution)/shard_map/mul | solution.py:29
  14.9 0.0 copy-done.1
  14.9 0.0 copy-done.2
  14.9 11.6 %fusion = bf16[4096,1024]{1,0:T(8,128)(2,1)S(1)} fusion(f32[512,8,8,128]{3,2,1,0:T(8,128)} %bitcast.15, bf16[4096,1024]{1,0:T(8,128)(2,1)} %param.5, bf16[4096,256]{1,0:T(8,128)(2,1)S(1)} %copy-done.1, bf16[1024,256]{1,0:T(8,128)(2,1)S(1)} %copy-done.2), kind=kOutput, calls=%fused_computation.1 | convolution fusion | flops 2168455168 | bytes 36175872 | tf_op jit(solution)/shard_map/dot_general | solution.py:24
  26.5 0.0 copy-start
  26.5 3.2 copy-done
  29.7 3.4 convolution_multiply_fusion.1
  33.1 0.0 all-reduce.5.cloned.1.call-update
  33.1 0.0 all-reduce.3.cloned.1.call-start
  33.1 7.7 %convolution_multiply_fusion = f32[4096,256]{1,0:T(8,128)} fusion(bf16[4096,1024]{1,0:T(8,128)(2,1)} %copy-done, bf16[1024,256]{1,0:T(8,128)(2,1)S(1)} %copy-done.2), kind=kOutput, calls=%fused_computation.2 | convolution fusion | flops 2148532224 | bytes 13107200 | tf_op jit(solution)/shard_map/dot_general | solution.py:33
  40.8 0.0 copy-start.4
  40.8 0.0 all-reduce.3.cloned.1.call-update
  40.9 3.8 %collective-permute-start = (bf16[96,256]{1,0:T(8,128)(2,1)S(1)}, bf16[96,256]{1,0:T(8,128)(2,1)S(1)}, u32[]{:S(2)}, u32[]{:S(2)}) collective-permute-start(bf16[96,256]{1,0:T(8,128)(2,1)S(1)} %slice.40), channel_id=1, source_target_pairs={{0,1},{1,2},{2,3},{3,4},{4,5},{5,6},{6,7},{7,8},{8,9},{9,10},{10,1... | collective-permute-start | bytes 147464 | tf_op jit(solution)/shard_map/ppermute | solution.py:15
  44.7 0.0 copy-done.4
  44.7 1.7 collective-permute-done
  46.4 0.1 maximum_convert_fusion
  46.5 0.3 fusion.12
  46.9 0.0 copy-start.3
  46.9 1.0 copy-done.3
  47.9 1.3 collective-permute-start.1
  49.1 5.0 %collective-permute-done.1 = bf16[96,256]{1,0:T(8,128)(2,1)S(1)} collective-permute-done((bf16[96,256]{1,0:T(8,128)(2,1)S(1)}, bf16[96,256]{1,0:T(8,128)(2,1)S(1)}, u32[]{:S(2)}, u32[]{:S(2)}) %collective-permute-start.1) | collective-permute-done | bytes 49184 | tf_op jit(solution)/shard_map/ppermute | solution.py:15
  54.2 101.0 %all-reduce.5.cloned.1.call-done = f32[1024,256]{1,0:T(8,128)} async-done(((f32[1024,256]{1,0:T(8,128)}), f32[1024,256]{1,0:T(8,128)}) %all-reduce.5.cloned.1.call-update) | async-done | bytes 1048592 | tf_op jit(solution)/shard_map/psum | solution.py:48
  155.2 4.3 %fusion.7 = bf16[1024,256]{1,0:T(8,128)(2,1)} fusion(f32[1024,256]{1,0:T(8,128)} %copy-done.3, f32[96,256]{1,0:T(8,128)S(1)} %convert_element_type.35, f32[1024,256]{1,0:T(8,128)} %all-reduce.5.cloned.1.call-done, bf16[1024,256]{1,0:T(8,128)(2,1)S(1)} %copy-done.2, f32[256]{0:T(256)S(1)} %bitcast.19, f32[256]{0:T(256)S(1)} %bitcast.21, f32[256]{0:T(256)S(1)} %bitcast.17), kind=kLoop, calls=%fused_computation.15 | loop fusion | flops 3932160 | bytes 3247104 | tf_op jit(solution)/shard_map/convert_element_type | solution.py:55
  159.5 179.3 %all-reduce.3.cloned.1.call-done = f32[4096,256]{1,0:T(8,128)} async-done(((f32[4096,256]{1,0:T(8,128)}), f32[4096,256]{1,0:T(8,128)}) %all-reduce.3.cloned.1.call-update) | async-done | bytes 4194320 | tf_op jit(solution)/shard_map/psum | solution.py:33
  338.8 4.1 %add_convert_fusion = bf16[4096,256]{1,0:T(8,128)(2,1)} fusion(f32[4096,256]{1,0:T(8,128)} %all-reduce.3.cloned.1.call-done, bf16[4096,256]{1,0:T(8,128)(2,1)S(1)} %copy-done.1), kind=kLoop, calls=%fused_computation.3 | loop fusion | flops 5242880 | bytes 8388608 | tf_op jit(solution)/shard_map/convert_element_type | solution.py:34
  (4 shorter events, 0.0 us)
Async XLA Ops:
  7.2 148.0 %all-reduce.5.cloned.1.call-start = ((), (), s32[]{:S(2)}) async-start(), calls=%async_computation.1 | async-start | bytes 2097152 | tf_op jit(solution)/shard_map/psum | solution.py:48
  8.0 6.9 %copy-start.1 = (bf16[4096,256]{1,0:T(8,128)(2,1)S(1)}, bf16[4096,256]{1,0:T(8,128)(2,1)}, u32[]{:S(2)}) copy-start(bf16[4096,256]{1,0:T(8,128)(2,1)} %param.7) | copy-start | bytes 6291460
  8.0 6.9 %copy-start.2 = (bf16[1024,256]{1,0:T(8,128)(2,1)S(1)}, bf16[1024,256]{1,0:T(8,128)(2,1)}, u32[]{:S(2)}) copy-start(bf16[1024,256]{1,0:T(8,128)(2,1)} %param.8) | copy-start | bytes 1572868
  26.5 3.2 copy-start
  33.1 305.7 %all-reduce.3.cloned.1.call-start = ((), (), s32[]{:S(2)}) async-start(), calls=%async_computation | async-start | bytes 8388608 | tf_op jit(solution)/shard_map/psum | solution.py:33
  40.8 3.9 %copy-start.4 = (f32[3,256]{1,0:T(4,128)S(1)}, f32[3,256]{1,0:T(4,128)}, u32[]{:S(2)}) copy-start(f32[3,256]{1,0:T(4,128)} %param.9) | copy-start | bytes 9220
  40.9 5.6 %collective-permute-start = (bf16[96,256]{1,0:T(8,128)(2,1)S(1)}, bf16[96,256]{1,0:T(8,128)(2,1)S(1)}, u32[]{:S(2)}, u32[]{:S(2)}) collective-permute-start(bf16[96,256]{1,0:T(8,128)(2,1)S(1)} %slice.40), channel_id=1, source_target_pairs={{0,1},{1,2},{2,3},{3,4},{4,5},{5,6},{6,7},{7,8},{8,9},{9,10},{10,1... | collective-permute-start | bytes 147464 | tf_op jit(solution)/shard_map/ppermute | solution.py:15
  46.9 1.0 copy-start.3
  47.9 6.3 %collective-permute-start.1 = (bf16[96,256]{1,0:T(8,128)(2,1)S(1)}, bf16[96,256]{1,0:T(8,128)(2,1)S(1)}, u32[]{:S(2)}, u32[]{:S(2)}) collective-permute-start(bf16[96,256]{1,0:T(8,128)(2,1)S(1)} %slice.106), channel_id=1, source_target_pairs={{1,0},{2,1},{3,2},{4,3},{5,4},{6,5},{7,6},{8,7},{9,8},{10,9},{11,1... | collective-permute-start | bytes 147464 | tf_op jit(solution)/shard_map/ppermute | solution.py:15
Sparse Core Ops, SparseCore 0:
  33.2 121.9 all-reduce.4
  158.1 180.6 all-reduce.2
where the time goes:
time: 350 us
  waiting for transfers between devices  287 us (82%)
  matrix products  22.6 us (6%)
  between operations  14.1 us (4%)
  local copies, waits for them, and re-layouts  11.2 us (3%)
  other arithmetic  9.51 us (3%)
  starting transfers between devices  5.18 us (1%)
    psum x1, waiting for transfers between devices, on_device(): lax.psum(jnp.dot(resid, time_f, preferred_element_type=jnp.float32) * sca...  179 us
    psum x1, waiting for transfers between devices, on_device(): lax.psum(lax.dot_general(resid, sensor_f, (((0,), (0,)), ((), ())), prefe...  101 us
    dot_general x1, matrix products, on_device(): jnp.dot(sensor_f, time_f.T, preferred_element_type=jnp.float32) * scale  11.6 us
    dot_general x1, matrix products, on_device(): jnp.dot(resid, time_f, preferred_element_type=jnp.float32) * scale  7.69 us
  transfers between devices with their start and end apart: 4, of which 4 were waited for; matrix products, arithmetic and copies ran while one was open for 4% of the time, Pallas kernels for 0%

commit v1 on v0

v1 whole, which is shorter than its diff:
```python
import functools
import math

import jax
import jax.numpy as jnp
from jax import lax
from jax.experimental import pallas as pl
from jax.experimental.pallas import tpu as pltpu
from jax.sharding import PartitionSpec as P

TILE = 128
LAG = 96
RANK = 256
GROUP = 4 * TILE
COLS = 256
MESH = pl.DeviceIdType.MESH
F32 = jnp.float32
BF16 = jnp.bfloat16
HALF = TILE // 2

PLACE = {4: 0, 3: 1, 5: 2, 2: 3, 6: 4, 1: 5, 7: 6, 0: 7}


def kernel(
    step_sens, step_time,
    rd_hbm, mask, sn_hbm, t_hbm, arw,
    outs_hbm, outt_hbm,
    rd, sn, tpad, g, gtt, s_t, resid, ysend, yrecv, zsend, zru, zrd, pxs, pxr, out,
    gt, core_in, xs, xr, acc, ys, yr, winf, errf, tout,
    load_sem, store_sem, send_sem, recv_sem,
):
    blk = lax.axis_index("blk")
    tm = lax.axis_index("tm")
    x, ylo, c = blk // 4, (blk // 2) % 2, blk % 2
    h, z = tm // 8, tm % 8

    def at_blk(x_, ylo_, c_):
        return ((x_ * 2 + ylo_) * 2 + c_, tm)

    up = (blk, h * 8 + (z + 1) % 8)
    down = (blk, h * 8 + (z + 7) % 8)
    pair = (blk, (1 - h) * 8 + z)
    after = (blk, (tm + 1) % 16)
    before = (blk, (tm + 15) % 16)
    other_core = at_blk(x, ylo, 1 - c)
    x_away = [None] + [at_blk((x + d) % 4, ylo, c) for d in (1, 2, 3)]
    y_next = at_blk(x, 1 - ylo, c)

    barrier = pltpu.get_barrier_semaphore()
    partners = [up, down, pair, after, before, other_core, y_next] + x_away[1:]
    for who in partners:
        pl.semaphore_signal(barrier, inc=1, device_id=who, device_id_type=MESH)

    t_rows = t_hbm.shape[0]
    t_load = pltpu.make_async_copy(t_hbm, tpad.at[pl.ds(LAG, t_rows)], load_sem.at[16])

    def rows_of(k):
        return pl.multiple_of(((z + k) % 8) * GROUP, GROUP)

    def owner_of(p):
        d = (p + 1) // 2
        return (z + 8 + 4 + d * (1 - 2 * (p % 2))) % 8

    def loads(p):
        r = pl.multiple_of(owner_of(p) * GROUP, GROUP)
        a = pltpu.make_async_copy(sn_hbm.at[pl.ds(r, GROUP)], sn.at[pl.ds(r, GROUP)], load_sem.at[p])
        b = pltpu.make_async_copy(rd_hbm.at[pl.ds(r, GROUP)], rd.at[pl.ds(r, GROUP)], load_sem.at[8 + p])
        return a, b

    t_load.start()
    for p in range(8):
        for cp in loads(p):
            cp.start()

    q_off = [h * TILE, (1 - h) * TILE, (2 + h) * TILE, (3 - h) * TILE]
    q_off = [pl.multiple_of(v, TILE) for v in q_off]

    def q_rows(q):
        return pl.ds(q_off[q], TILE)

    count = [8]
    sent = []

    def message(src, dst, who):
        n = count[0]
        count[0] += 1
        return pltpu.make_async_remote_copy(
            src_ref=src, dst_ref=dst, send_sem=send_sem.at[n], recv_sem=recv_sem.at[n],
            device_id=who, device_id_type=MESH,
        )

    def start(msg):
        msg.start()
        sent.append(msg)

    def y_message(p):
        return pltpu.make_async_remote_copy(
            src_ref=ysend.at[p], dst_ref=yrecv.at[p], send_sem=send_sem.at[p], recv_sem=recv_sem.at[p],
            device_id=pair, device_id_type=MESH,
        )

    gtt[...] = jnp.zeros_like(gtt)

    def compute(p):
        o = owner_of(p)
        r = pl.multiple_of(o * GROUP, GROUP)
        for cp in loads(p):
            cp.wait()
        s = sn[pl.ds(r, GROUP), :]
        s_t[...] = s.T
        g[p] = jnp.zeros((GROUP, RANK), F32)

        def columns(j, carry):
            col = pl.multiple_of(j * COLS, COLS)
            tj = tpad[pl.ds(LAG + col, COLS), :]
            pred = lax.dot_general(
                sn[pl.ds(r, GROUP), :], tj, (((1,), (1,)), ((), ())), preferred_element_type=F32
            )
            diff = rd[pl.ds(r, GROUP), pl.ds(col, COLS)].astype(F32) - pred * (1.0 / math.sqrt(RANK))
            for i in range(GROUP // TILE):
                for jj in range(COLS // TILE):
                    keep = mask[o * (GROUP // TILE) + i, j * (COLS // TILE) + jj].astype(F32)
                    block = diff[i * TILE : (i + 1) * TILE, jj * TILE : (jj + 1) * TILE]
                    resid[i * TILE : (i + 1) * TILE, jj * TILE : (jj + 1) * TILE] = (block * keep).astype(BF16)
            left = resid[...]
            g[p] += jnp.dot(left, tj, preferred_element_type=F32)
            gtt[:, pl.ds(col, COLS)] += jnp.dot(s_t[...], left, preferred_element_type=F32)
            return carry

        lax.fori_loop(0, t_rows // COLS, columns, 0)

    def y_first(p):
        ysend[p] = g[p, q_rows(3), :].astype(BF16)
        y_message(p).start()

    def compute_some(first, last):
        def one(p, carry):
            compute(p)
            y_first(p)
            return carry

        lax.fori_loop(first, last, one, 0)

    z_up, z_down = {}, {}
    for k in (4, 3, 2, 1):
        for q in range(3):
            p, p_down = PLACE[k], PLACE[(8 - k) % 8]
            a, b = q * TILE, (q + 1) * TILE
            if k == 4:
                if q == 0:
                    z_up[k, q] = message(zsend.at[p, a:b], zru.at[k - 1, a:b], up)
                elif q == 1:
                    z_down[k, q] = message(zsend.at[p, a:b], zrd.at[k - 1, a:b], down)
                else:
                    z_up[k, q] = message(zsend.at[p, a : a + HALF], zru.at[k - 1, a : a + HALF], up)
                    z_down[k, q] = message(zsend.at[p, a + HALF : b], zrd.at[k - 1, a + HALF : b], down)
            else:
                z_up[k, q] = message(zsend.at[p, a:b], zru.at[k - 1, a:b], up)
                z_down[k, q] = message(zsend.at[p_down, a:b], zrd.at[k - 1, a:b], down)

    def own(p, q):
        part = g[p, q_rows(q), :]
        if q == 2:
            part = part + yrecv[p].astype(F32)
        return part

    def pass_on(k, q, upward):
        p = PLACE[k] if upward else PLACE[(8 - k) % 8]
        a, b = q * TILE, (q + 1) * TILE
        table, landed = (z_up, zru) if upward else (z_down, zrd)
        if q == 2 and (k == 4 and upward or k < 4):
            y_message(p).wait_recv()
        part = own(p, q)
        if k < 4 and (k + 1, q) in table:
            table[k + 1, q].wait_recv()
            if k == 3 and q == 2:
                if upward:
                    lo = part[:HALF] + landed[k, a : a + HALF].astype(F32)
                    part = jnp.concatenate([lo, part[HALF:]], axis=0)
                else:
                    hi = part[HALF:] + landed[k, a + HALF : b].astype(F32)
                    part = jnp.concatenate([part[:HALF], hi], axis=0)
            else:
                part = part + landed[k, a:b].astype(F32)
        if k == 4 and q == 2:
            if upward:
                zsend[p, a : a + HALF] = part[:HALF].astype(BF16)
            else:
                zsend[p, a + HALF : b] = part[HALF:].astype(BF16)
        else:
            zsend[p, a:b] = part.astype(BF16)
        start(table[k, q])

    t_load.wait()
    compute(0)
    pl.semaphore_wait(barrier, len(partners))
    y_first(0)
    pass_on(4, 0, True)
    pass_on(4, 1, False)
    rim_up = message(tpad.at[pl.ds(t_rows, LAG)], tpad.at[pl.ds(0, LAG)], after)
    rim_down = message(tpad.at[pl.ds(LAG, LAG)], tpad.at[pl.ds(LAG + t_rows, LAG)], before)
    start(rim_up)
    start(rim_down)
    compute_some(1, 3)
    pass_on(3, 1, True)
    pass_on(3, 0, False)
    pass_on(4, 2, True)
    pass_on(4, 2, False)
    pass_on(3, 0, True)
    pass_on(3, 1, False)
    compute_some(3, 5)
    pass_on(3, 2, True)
    pass_on(3, 2, False)
    for q in (1, 0):
        pass_on(2, q, True)
        pass_on(2, 1 - q, False)
    compute_some(5, 8)

    for j in range(t_rows // COLS):
        gt[j * COLS : (j + 1) * COLS, :] = gtt[:, j * COLS : (j + 1) * COLS].T
    half_t = t_rows // 2
    per_x = half_t // 4
    per_y = per_x // 2
    mine = pl.multiple_of(c * half_t, half_t)
    theirs = pl.multiple_of((1 - c) * half_t, half_t)
    core_msg = message(gt.at[pl.ds(theirs, half_t)], core_in, other_core)
    start(core_msg)

    pass_on(2, 2, True)
    pass_on(2, 2, False)
    for q in (1, 0):
        pass_on(1, q, True)
        pass_on(1, 1 - q, False)

    def x_rows(d):
        return pl.multiple_of(((x + d) % 4) * per_x, per_x)

    core_msg.wait_recv()
    x_msgs = []
    for d in (1, 2, 3):
        r = x_rows(d)
        xs[d - 1] = (gt[pl.ds(mine + r, per_x), :] + core_in[pl.ds(r, per_x), :]).astype(BF16)
        msg = message(xs.at[d - 1], xr.at[d - 1], x_away[d])
        start(msg)
        x_msgs.append(msg)
    r = x_rows(0)
    acc[...] = gt[pl.ds(mine + r, per_x), :] + core_in[pl.ds(r, per_x), :]

    pass_on(1, 2, True)
    pass_on(1, 2, False)

    def z_total(q):
        if q == 2:
            y_message(7).wait_recv()
        part = own(7, q)
        a, b = q * TILE, (q + 1) * TILE
        z_up[1, q].wait_recv()
        part = part + zru[0, a:b].astype(F32)
        z_down[1, q].wait_recv()
        return part + zrd[0, a:b].astype(F32)

    def out_rows(k, q):
        return pl.multiple_of(rows_of(k) + q_off[q], TILE)

    def finished(q, total):
        r = out_rows(0, q)
        sensors = sn[pl.ds(r, TILE), :].astype(F32)
        out[pl.ds(r, TILE), :] = (0.9 * sensors + (step_sens / math.sqrt(RANK)) * total).astype(BF16)

    g_up, g_down, g_pair = {}, {}, {}

    def hand_on(s, q):
        for upward in (True, False):
            k = (8 - (s - 1)) % 8 if upward else s - 1
            r = out_rows(k, q)
            table, who = (g_up, up) if upward else (g_down, down)
            size = TILE
            if s == 4:
                if q == 0 and not upward or q == 1 and upward:
                    continue
                if q == 2:
                    size = HALF
                    r = r if upward else r + HALF
            if s > 1:
                table[s - 1, q].wait_recv()
            rows = out.at[pl.ds(r, size)]
            table[s, q] = message(rows, rows, who)
            start(table[s, q])
            if q == 2 and (s == 1 and upward or s > 1):
                across(k, (8 - k) % 8 if k else 0)

    def across(k, label):
        r = out_rows(k, 2)
        rows = out.at[pl.ds(r, TILE)]
        g_pair[k] = message(rows, rows, pair)
        start(g_pair[k])

    pxs[...] = z_total(1).astype(BF16)
    px_msg = message(pxs, pxr, pair)
    start(px_msg)
    g[7, q_rows(0), :] = z_total(0)
    finished(2, z_total(2))
    hand_on(1, 2)

    for msg in x_msgs:
        msg.wait_recv()
    acc[...] += (xr[0].astype(F32) + xr[1].astype(F32)) + xr[2].astype(F32)
    ys[...] = acc[pl.ds(pl.multiple_of((1 - ylo) * per_y, per_y), per_y), :].astype(BF16)
    y_msg = message(ys, yr, y_next)
    start(y_msg)

    px_msg.wait_recv()
    finished(0, g[7, q_rows(0), :] + pxr[...].astype(F32))
    r0 = out_rows(0, 0)
    fin_msg = message(out.at[pl.ds(r0, TILE)], out.at[pl.ds(r0, TILE)], pair)
    start(fin_msg)
    hand_on(1, 0)
    hand_on(2, 2)

    rim_up.wait_recv()
    rim_down.wait_recv()
    y_msg.wait_recv()
    first = pl.multiple_of(mine + x_rows(0) + ylo * per_y, per_y)
    seen = per_y + 2 * LAG
    win = tpad[pl.ds(first, seen), :].astype(F32)
    step = first - LAG + lax.broadcasted_iota(jnp.int32, (seen, RANK), 0)
    winf[...] = jnp.where((step >= 0) | (tm > 0), win, 0.0)
    errs = per_y + LAG
    err = winf[LAG : LAG + errs, :]
    lags = (1, 12, LAG)
    for i in range(3):
        err = err - arw[i : i + 1, :] * winf[LAG - lags[i] : LAG - lags[i] + errs, :]
    step = first + lax.broadcasted_iota(jnp.int32, (errs, RANK), 0)
    errf[...] = jnp.where((step < t_rows) | (tm < 15), err, 0.0)
    adj = errf[0:per_y, :]
    for i in range(3):
        adj = adj - arw[i : i + 1, :] * errf[lags[i] : lags[i] + per_y, :]
    total = acc[pl.ds(pl.multiple_of(ylo * per_y, per_y), per_y), :] + yr[...].astype(F32)
    new = winf[LAG : LAG + per_y, :] + (step_time / math.sqrt(RANK)) * total - 0.5 * adj
    tout[pl.ds(first, per_y), :] = new.astype(BF16)
    ty_rows = tout.at[pl.ds(first, per_y)]
    ty_msg = message(ty_rows, ty_rows, y_next)
    start(ty_msg)

    fin_msg.wait_recv()
    hand_on(1, 1)
    hand_on(2, 0)
    hand_on(3, 2)
    ty_msg.wait_recv()
    tx_rows = tout.at[pl.ds(pl.multiple_of(mine + x_rows(0), per_x), per_x)]
    tx_msgs = []
    for d in (1, 2, 3):
        msg = message(tx_rows, tx_rows, x_away[d])
        start(msg)
        tx_msgs.append(msg)
    hand_on(2, 1)
    hand_on(3, 0)
    hand_on(4, 2)
    hand_on(3, 1)
    hand_on(4, 0)
    hand_on(4, 1)
    for msg in tx_msgs:
        msg.wait_recv()
    tc_rows = tout.at[pl.ds(mine, half_t)]
    tc_msg = message(tc_rows, tc_rows, other_core)
    start(tc_msg)

    g_up[4, 2].wait_recv()
    g_down[4, 2].wait_recv()
    across(4, 4)
    stores = []

    def store(src, dst):
        cp = pltpu.make_async_copy(src, dst, store_sem.at[len(stores)])
        cp.start()
        stores.append(cp)

    tc_msg.wait_recv()
    store(tout, outt_hbm)
    g_up[4, 0].wait_recv()
    g_down[4, 1].wait_recv()
    for s in (3,):
        for q in (0, 1):
            if q == 0:
                g_down[3, 0].wait_recv()
            else:
                g_up[3, 1].wait_recv()
    for k in (0, 7, 1, 6, 2, 5, 3, 4):
        g_pair[k].wait_recv()
        rows = pl.ds(rows_of(k), GROUP)
        store(out.at[rows], outs_hbm.at[rows])
    for p in range(8):
        y_message(p).wait_send()
    for msg in sent:
        msg.wait_send()
    for cp in stores:
        cp.wait()


def on_device(readings, tile_mask, sensor_f, time_f, ar_weight):
    sens_here, time_here = readings.shape
    time_total = time_here * lax.axis_size("tm")
    sens_total = sens_here * lax.axis_size("blk")
    rank = sensor_f.shape[1]
    step_sens = 2.0 * math.sqrt(rank / time_total)
    step_time = 2.0 * math.sqrt(rank / sens_total)
    half_t = time_here // 2
    per_x = half_t // 4
    per_y = per_x // 2
    anywhere = pl.BlockSpec(memory_space=pl.ANY)
    in_vmem = pl.BlockSpec(memory_space=pltpu.VMEM)
    messages = 100
    flops = 6 * sens_here * time_here * rank
    return pl.pallas_call(
        functools.partial(kernel, step_sens, step_time),
        out_shape=(
            jax.ShapeDtypeStruct(sensor_f.shape, BF16),
            jax.ShapeDtypeStruct(time_f.shape, BF16),
        ),
        in_specs=[anywhere, pl.BlockSpec(memory_space=pltpu.SMEM), anywhere, anywhere, in_vmem],
        out_specs=(anywhere, anywhere),
        scratch_shapes=[
            pltpu.VMEM((sens_here, time_here), BF16),
            pltpu.VMEM((sens_here, rank), BF16),
            pltpu.VMEM((time_here + 2 * LAG, rank), BF16),
            pltpu.VMEM((8, GROUP, rank), F32),
            pltpu.VMEM((rank, time_here), F32),
            pltpu.VMEM((rank, GROUP), BF16),
            pltpu.VMEM((GROUP, COLS), BF16),
            pltpu.VMEM((8, TILE, rank), BF16),
            pltpu.VMEM((8, TILE, rank), BF16),
            pltpu.VMEM((8, 3 * TILE, rank), BF16),
            pltpu.VMEM((4, 3 * TILE, rank), BF16),
            pltpu.VMEM((4, 3 * TILE, rank), BF16),
            pltpu.VMEM((TILE, rank), BF16),
            pltpu.VMEM((TILE, rank), BF16),
            pltpu.VMEM((sens_here, rank), BF16),
            pltpu.VMEM((time_here, rank), F32),
            pltpu.VMEM((half_t, rank), F32),
            pltpu.VMEM((3, per_x, rank), BF16),
            pltpu.VMEM((3, per_x, rank), BF16),
            pltpu.VMEM((per_x, rank), F32),
            pltpu.VMEM((per_y, rank), BF16),
            pltpu.VMEM((per_y, rank), BF16),
            pltpu.VMEM((per_y + 2 * LAG, rank), F32),
            pltpu.VMEM((per_y + LAG, rank), F32),
            pltpu.VMEM((time_here, rank), BF16),
            pltpu.SemaphoreType.DMA((17,)),
            pltpu.SemaphoreType.DMA((9,)),
            pltpu.SemaphoreType.DMA((messages,)),
            pltpu.SemaphoreType.DMA((messages,)),
        ],
        compiler_params=pltpu.CompilerParams(
            collective_id=0, has_side_effects=True, vmem_limit_bytes=48 * 1024 * 1024
        ),
        cost_estimate=pl.CostEstimate(
            flops=flops, bytes_accessed=2 * sens_here * time_here, transcendentals=0
        ),
        name="sweep",
    )(readings, tile_mask, sensor_f, time_f, ar_weight)


def solution(mesh):
    return jax.shard_map(
        on_device,
        mesh=mesh,
        in_specs=(P("blk", "tm"), P("blk", "tm"), P("blk", None), P("tm", None), P()),
        out_specs=(P("blk", None), P("tm", None)),
        check_vma=False,
    )
```

time: 350 us -> 70.1 us (0.20)
  waiting for transfers between devices: 287 us -> 0 us
  Pallas kernels: 0 us -> 63 us
  matrix products: 22.6 us -> 0 us
  between operations: 14.1 us -> 0.64 us
  other arithmetic: 9.51 us -> 0 us
  starting transfers between devices: 5.18 us -> 0 us
  local copies, waits for them, and re-layouts: 11.2 us -> 6.19 us
    psum x2 -> x0, waiting for transfers between devices: 280 us -> none  [the longest x1 179 us: on_device(): lax.psum(jnp.dot(resid, time_f, preferred_element_type=jnp.float32) * sca...]
    pallas_call x0 -> x1, Pallas kernels: none -> 63 us  [on_device(): pl.pallas_call(functools.partial(kernel, step_sens, step_time), out_shape...]
    dot_general x3 -> x0, matrix products: 22.6 us -> none  [the longest x1 11.6 us: on_device(): jnp.dot(sensor_f, time_f.T, preferred_element_type=jnp.float32) * scale]
    convert_element_type x5 -> x0, other arithmetic: 9.16 us -> none  [the longest x1 4.26 us: on_device(): (factor + step_time * grad_t - 0.5 * ar_adj).astype(jnp.bfloat16)]
    mul x1 -> x0, local copies, waits for them, and re-layouts: 6.88 us -> none  [on_device(): resid = (diff * keep).reshape(sens_here, time_here).astype(jnp.bfloat16)]
    ppermute x2 -> x0, waiting for transfers between devices: 6.72 us -> none  [passed_along(): return lax.ppermute(block, axis, route)]
    ppermute x2 -> x0, starting transfers between devices: 5.1 us -> none  [passed_along(): return lax.ppermute(block, axis, route)]
  transfers between devices with their start and end apart: 4 -> 0, of which waited for: 4 -> 0; matrix products, arithmetic and copies ran while one was open for 4% -> 0% of each run, Pallas kernels for 0% -> 0%
where the time goes in v1:
time: 70.1 us; the launch traced here: 69.8 us
  Pallas kernels  63 us (90%)
  local copies, waits for them, and re-layouts  6.19 us (9%)
    pallas_call x1, Pallas kernels, on_device(): pl.pallas_call(functools.partial(kernel, step_sens, step_time), out_shape...  63 us
    unnamed x9, local copies, waits for them, and re-layouts  6.19 us

profile of v1, /device:TPU:2, one launch (start us, length us, event | category | flops | bytes accessed | tf_op | source)
XLA Modules:
  0.0 69.8 jit_solution(11130760419230071865)
XLA Ops:
  0.6 0.8 %copy.7.mask = s32[32,8]{1,0:T(8,128)S(1)} copy(s32[32,8]{0,1:T(8,128)} %param.6) | data formatting | bytes 2048 | tf_op args[1]
  1.4 0.0 copy-start
  1.4 1.6 %copy-done = bf16[4096,256]{1,0:T(8,128)(2,1)S(1)} copy-done((bf16[4096,256]{1,0:T(8,128)(2,1)S(1)}, bf16[4096,256]{1,0:T(8,128)(2,1)}, u32[]{:S(2)}) %copy-start) | copy-done | bytes 2097176
  3.0 0.0 copy-start.1
  3.0 1.0 %copy-done.1 = bf16[1024,256]{1,0:T(8,128)(2,1)S(1)} copy-done((bf16[1024,256]{1,0:T(8,128)(2,1)S(1)}, bf16[1024,256]{1,0:T(8,128)(2,1)}, u32[]{:S(2)}) %copy-start.1) | copy-done | bytes 524312
  4.0 0.0 copy-start.2
  4.0 0.7 copy-done.2
  4.7 63.0 %sweep.1 = (bf16[4096,256]{1,0:T(8,128)(2,1)S(1)}, bf16[1024,256]{1,0:T(8,128)(2,1)S(1)}) custom-call(bf16[4096,1024]{1,0:T(8,128)(2,1)} %rd_hbm.1, s32[32,8]{1,0:T(8,128)S(1)} %copy.7.mask, bf16[4096,256]{1,0:T(8,128)(2,1)S(1)} %copy-done, bf16[1024,256]{1,0:T(8,128)(2,1)S(1)} %copy-done.1, f32[3,256]{1,0:T(4,128)S(1)} %copy-done.2), custom_call_target="tpu_custom_call" | custom-call | flops 6442450944 | bytes 8388608 | tf_op jit(solution)/shard_map/sweep/pallas_call | solution.py:414
  67.7 1.3 %copy.10 = bf16[4096,256]{1,0:T(8,128)(2,1)} copy(bf16[4096,256]{1,0:T(8,128)(2,1)S(1)} %get-tuple-element.4) | data formatting | bytes 4194304
  69.1 0.8 %copy.11 = bf16[1024,256]{1,0:T(8,128)(2,1)} copy(bf16[1024,256]{1,0:T(8,128)(2,1)S(1)} %get-tuple-element.5) | data formatting | bytes 1048576
Async XLA Ops:
  1.4 1.6 %copy-start = (bf16[4096,256]{1,0:T(8,128)(2,1)S(1)}, bf16[4096,256]{1,0:T(8,128)(2,1)}, u32[]{:S(2)}) copy-start(bf16[4096,256]{1,0:T(8,128)(2,1)} %sn_hbm.1) | copy-start | bytes 6291460
  3.0 1.0 %copy-start.1 = (bf16[1024,256]{1,0:T(8,128)(2,1)S(1)}, bf16[1024,256]{1,0:T(8,128)(2,1)}, u32[]{:S(2)}) copy-start(bf16[1024,256]{1,0:T(8,128)(2,1)} %t_hbm.1) | copy-start | bytes 1572868
  4.0 0.7 copy-start.2

commit v2 on v1

--- a/solution.py
+++ b/solution.py
@@ -23,11 +23,11 @@
 
 def kernel(
     step_sens, step_time,
-    rd_hbm, mask, sn_hbm, t_hbm, arw,
-    outs_hbm, outt_hbm,
-    rd, sn, tpad, g, gtt, s_t, resid, ysend, yrecv, zsend, zru, zrd, pxs, pxr, out,
-    gt, core_in, xs, xr, acc, ys, yr, winf, errf, tout,
-    load_sem, store_sem, send_sem, recv_sem,
+    rd_hbm, mask_hbm, sn_hbm, t_hbm, arw_hbm,
+    out, tout,
+    mask, arw, rd, sn, tpad, t_t, g, gtt, s_t, resid, ysend, yrecv, zsend, zru, zrd, pxs, pxr,
+    gt, core_in, xs, xr, acc, ys, yr, winf, errf,
+    load_sem, send_sem, recv_sem,
 ):
     blk = lax.axis_index("blk")
     tm = lax.axis_index("tm")
@@ -67,10 +67,14 @@
         b = pltpu.make_async_copy(rd_hbm.at[pl.ds(r, GROUP)], rd.at[pl.ds(r, GROUP)], load_sem.at[8 + p])
         return a, b
 
+    mask_load = pltpu.make_async_copy(mask_hbm, mask, load_sem.at[17])
+    arw_load = pltpu.make_async_copy(arw_hbm, arw, load_sem.at[18])
     t_load.start()
+    mask_load.start()
     for p in range(8):
         for cp in loads(p):
             cp.start()
+    arw_load.start()
 
     q_off = [h * TILE, (1 - h) * TILE, (2 + h) * TILE, (3 - h) * TILE]
     q_off = [pl.multiple_of(v, TILE) for v in q_off]
@@ -106,28 +110,19 @@
         r = pl.multiple_of(o * GROUP, GROUP)
         for cp in loads(p):
             cp.wait()
-        s = sn[pl.ds(r, GROUP), :]
-        s_t[...] = s.T
-        g[p] = jnp.zeros((GROUP, RANK), F32)
-
-        def columns(j, carry):
-            col = pl.multiple_of(j * COLS, COLS)
-            tj = tpad[pl.ds(LAG + col, COLS), :]
-            pred = lax.dot_general(
-                sn[pl.ds(r, GROUP), :], tj, (((1,), (1,)), ((), ())), preferred_element_type=F32
-            )
-            diff = rd[pl.ds(r, GROUP), pl.ds(col, COLS)].astype(F32) - pred * (1.0 / math.sqrt(RANK))
+        s_t[...] = sn[pl.ds(r, GROUP), :].T
+        for j in range(t_rows // COLS):
+            cols = slice(j * COLS, (j + 1) * COLS)
+            pred = jnp.dot(sn[pl.ds(r, GROUP), :], t_t[:, cols], preferred_element_type=F32)
+            diff = rd[pl.ds(r, GROUP), cols].astype(F32) - pred * (1.0 / math.sqrt(RANK))
             for i in range(GROUP // TILE):
                 for jj in range(COLS // TILE):
-                    keep = mask[o * (GROUP // TILE) + i, j * (COLS // TILE) + jj].astype(F32)
+                    keep = mask[j * (COLS // TILE) + jj, o * (GROUP // TILE) + i].astype(F32)
                     block = diff[i * TILE : (i + 1) * TILE, jj * TILE : (jj + 1) * TILE]
-                    resid[i * TILE : (i + 1) * TILE, jj * TILE : (jj + 1) * TILE] = (block * keep).astype(BF16)
-            left = resid[...]
-            g[p] += jnp.dot(left, tj, preferred_element_type=F32)
-            gtt[:, pl.ds(col, COLS)] += jnp.dot(s_t[...], left, preferred_element_type=F32)
-            return carry
-
-        lax.fori_loop(0, t_rows // COLS, columns, 0)
+                    a, b = i * TILE, j * COLS + jj * TILE
+                    resid[a : a + TILE, b : b + TILE] = (block * keep).astype(BF16)
+        g[p] = jnp.dot(resid[...], tpad[LAG : LAG + t_rows, :], preferred_element_type=F32)
+        gtt[...] += jnp.dot(s_t[...], resid[...], preferred_element_type=F32)
 
     def y_first(p):
         ysend[p] = g[p, q_rows(3), :].astype(BF16)
@@ -192,6 +187,8 @@
         start(table[k, q])
 
     t_load.wait()
+    t_t[...] = tpad[LAG : LAG + t_rows, :].T
+    mask_load.wait()
     compute(0)
     pl.semaphore_wait(barrier, len(partners))
     y_first(0)
@@ -317,6 +314,7 @@
     hand_on(1, 0)
     hand_on(2, 2)
 
+    arw_load.wait()
     rim_up.wait_recv()
     rim_down.wait_recv()
     y_msg.wait_recv()
@@ -368,33 +366,17 @@
     g_up[4, 2].wait_recv()
     g_down[4, 2].wait_recv()
     across(4, 4)
-    stores = []
-
-    def store(src, dst):
-        cp = pltpu.make_async_copy(src, dst, store_sem.at[len(stores)])
-        cp.start()
-        stores.append(cp)
-
     tc_msg.wait_recv()
-    store(tout, outt_hbm)
     g_up[4, 0].wait_recv()
     g_down[4, 1].wait_recv()
-    for s in (3,):
-        for q in (0, 1):
-            if q == 0:
-                g_down[3, 0].wait_recv()
-            else:
-                g_up[3, 1].wait_recv()
+    g_down[3, 0].wait_recv()
+    g_up[3, 1].wait_recv()
     for k in (0, 7, 1, 6, 2, 5, 3, 4):
         g_pair[k].wait_recv()
-        rows = pl.ds(rows_of(k), GROUP)
-        store(out.at[rows], outs_hbm.at[rows])
     for p in range(8):
         y_message(p).wait_send()
     for msg in sent:
         msg.wait_send()
-    for cp in stores:
-        cp.wait()
 
 
 def on_device(readings, tile_mask, sensor_f, time_f, ar_weight):
@@ -407,26 +389,28 @@
     half_t = time_here // 2
     per_x = half_t // 4
     per_y = per_x // 2
-    anywhere = pl.BlockSpec(memory_space=pl.ANY)
     in_vmem = pl.BlockSpec(memory_space=pltpu.VMEM)
     messages = 100
     flops = 6 * sens_here * time_here * rank
     return pl.pallas_call(
         functools.partial(kernel, step_sens, step_time),
         out_shape=(
-            jax.ShapeDtypeStruct(sensor_f.shape, BF16),
-            jax.ShapeDtypeStruct(time_f.shape, BF16),
+            pltpu.VMEM(sensor_f.shape, BF16),
+            pltpu.VMEM(time_f.shape, BF16),
         ),
-        in_specs=[anywhere, pl.BlockSpec(memory_space=pltpu.SMEM), anywhere, anywhere, in_vmem],
-        out_specs=(anywhere, anywhere),
+        in_specs=[pl.BlockSpec(memory_space=pltpu.HBM)] * 5,
+        out_specs=(in_vmem, in_vmem),
         scratch_shapes=[
+            pltpu.SMEM((time_here // TILE, sens_here // TILE), jnp.int32),
+            pltpu.VMEM((3, rank), F32),
             pltpu.VMEM((sens_here, time_here), BF16),
             pltpu.VMEM((sens_here, rank), BF16),
             pltpu.VMEM((time_here + 2 * LAG, rank), BF16),
+            pltpu.VMEM((rank, time_here), BF16),
             pltpu.VMEM((8, GROUP, rank), F32),
             pltpu.VMEM((rank, time_here), F32),
             pltpu.VMEM((rank, GROUP), BF16),
-            pltpu.VMEM((GROUP, COLS), BF16),
+            pltpu.VMEM((GROUP, time_here), BF16),
             pltpu.VMEM((8, TILE, rank), BF16),
             pltpu.VMEM((8, TILE, rank), BF16),
             pltpu.VMEM((8, 3 * TILE, rank), BF16),
@@ -434,7 +418,6 @@
             pltpu.VMEM((4, 3 * TILE, rank), BF16),
             pltpu.VMEM((TILE, rank), BF16),
             pltpu.VMEM((TILE, rank), BF16),
-            pltpu.VMEM((sens_here, rank), BF16),
             pltpu.VMEM((time_here, rank), F32),
             pltpu.VMEM((half_t, rank), F32),
             pltpu.VMEM((3, per_x, rank), BF16),
@@ -444,9 +427,7 @@
             pltpu.VMEM((per_y, rank), BF16),
             pltpu.VMEM((per_y + 2 * LAG, rank), F32),
             pltpu.VMEM((per_y + LAG, rank), F32),
-            pltpu.VMEM((time_here, rank), BF16),
-            pltpu.SemaphoreType.DMA((17,)),
-            pltpu.SemaphoreType.DMA((9,)),
+            pltpu.SemaphoreType.DMA((19,)),
             pltpu.SemaphoreType.DMA((messages,)),
             pltpu.SemaphoreType.DMA((messages,)),
         ],
@@ -457,7 +438,7 @@
             flops=flops, bytes_accessed=2 * sens_here * time_here, transcendentals=0
         ),
         name="sweep",
-    )(readings, tile_mask, sensor_f, time_f, ar_weight)
+    )(*[pltpu.with_memory_space_constraint(v, pltpu.HBM) for v in (readings, tile_mask.T, sensor_f, time_f, ar_weight)])
 
 
 def solution(mesh):

time: 70.1 us -> 57.2 us (0.82)
  Pallas kernels: 63 us -> 54.3 us
  local copies, waits for them, and re-layouts: 6.19 us -> 2.11 us
    pallas_call x1, Pallas kernels: 63 us -> 54.3 us  [on_device(): pl.pallas_call(functools.partial(kernel, step_sens, step_time), out_shape...]
    unnamed x9 -> x2, local copies, waits for them, and re-layouts: 6.19 us -> 2.11 us
where the time goes in v2:
time: 57.2 us; the launch traced here: 57.1 us
  Pallas kernels  54.3 us (95%)
  local copies, waits for them, and re-layouts  2.11 us (4%)
  between operations  0.64 us (1%)
    pallas_call x1, Pallas kernels, on_device(): pl.pallas_call(functools.partial(kernel, step_sens, step_time), out_shape...  54.3 us
    unnamed x2, local copies, waits for them, and re-layouts  2.11 us

profile of v2, /device:TPU:2, one launch (start us, length us, event | category | flops | bytes accessed | tf_op | source)
XLA Modules:
  0.0 57.1 jit_solution(6928078404198625913)
XLA Ops:
  0.6 54.3 %sweep.1 = (bf16[4096,256]{1,0:T(8,128)(2,1)S(1)}, bf16[1024,256]{1,0:T(8,128)(2,1)S(1)}) custom-call(bf16[4096,1024]{1,0:T(8,128)(2,1)} %rd_hbm.1, s32[8,32]{1,0:T(8,128)} %bitcast.1, bf16[4096,256]{1,0:T(8,128)(2,1)} %sn_hbm.1, bf16[1024,256]{1,0:T(8,128)(2,1)} %t_hbm.1, f32[3,256]{1,0:T(4,128)} %arw_hbm.1), custom_call_target="tpu_custom_call" | custom-call | flops 6442450944 | bytes 8388608 | tf_op jit(solution)/shard_map/sweep/pallas_call | solution.py:395
  55.0 1.3 %copy.9 = bf16[4096,256]{1,0:T(8,128)(2,1)} copy(bf16[4096,256]{1,0:T(8,128)(2,1)S(1)} %get-tuple-element.2) | data formatting | bytes 4194304
  56.3 0.8 %copy.10 = bf16[1024,256]{1,0:T(8,128)(2,1)} copy(bf16[1024,256]{1,0:T(8,128)(2,1)S(1)} %get-tuple-element.3) | data formatting | bytes 1048576

commit v3 on v0

v3 whole, which is shorter than its diff:
```python
import functools
import math

import jax
import jax.numpy as jnp
from jax import lax
from jax.experimental import pallas as pl
from jax.experimental.pallas import tpu as pltpu
from jax.sharding import PartitionSpec as P

TILE = 128
LAG = 96
RANK = 256
GROUP = 4 * TILE
HALF = 2 * TILE
PIECE = TILE // 2
COLS = 256
MESSAGES = 105
MESH = pl.DeviceIdType.MESH
F32 = jnp.float32
BF16 = jnp.bfloat16

PLACE = {4: 0, 3: 1, 5: 2, 2: 3, 6: 4, 1: 5, 7: 6, 0: 7}

ORDER = (
    "a0", "r41d0", "b0", "y01", "r40u1", "a1", "r41d1", "y00", "r40u0", "b1", "a2", "r30d0", "r31u0", "y11",
    "r31u1", "b2", "r30d1", "y21", "y20", "a3", "r31d0", "r30u1", "b3", "r42d1", "r30u0", "r31d1", "y10",
    "r42u0", "a4", "y31", "r21u0", "b4", "r32u1", "r20d0", "y41", "a5", "r21u1", "y30", "r21d0", "b5",
    "r32d1", "r20u1", "a6", "r21d1", "r32d0", "y40", "r32u0", "b6", "r20d1", "y61", "r20u0", "y51", "r11u0",
    "a7", "y50", "y60", "r11d0", "r22u1", "b7", "r22d1", "r11u1", "r11d1", "g0", "r22u0", "r22d0", "r10d0",
    "y71", "r10u0", "s10", "y70", "r12u1", "r12d1", "r10u1", "r10d1", "g1", "s11", "r12u0", "r12d0", "s00",
    "f0", "s21", "h12d1", "h12u1", "x0u1", "h10u0", "h10d0", "s01", "s20", "h12d0", "h12u0", "f1", "h10d1",
    "x0u0", "h10u1", "x1d1", "h22u1", "h22d1", "g2", "h11u0", "h11d0", "h22u0", "h22d0", "x1d0", "x1u1",
    "h20u1", "h11d1", "h20d1", "h11u1", "h32d1", "h32u1", "x2d1", "g3", "x2u1", "h21d0", "h32u0", "h20u0",
    "h21d1", "h30u1", "h32d0", "h20d0", "x2d0", "x1u0", "h21u1", "h42d1", "x3d1", "h21u0", "g4", "x2u0",
    "h42u0", "h31d0", "x3u0", "h30u0", "h31d1", "h30d1", "x3d0", "h31u1", "h30d0", "x3u1", "h31u0", "x4d1",
    "h40u1", "h41d0", "x4u0", "h40u0", "h41d1", "g5",
)


def kernel(
    step_sens, step_time,
    rd_hbm, mask_hbm, sn_hbm, t_hbm, arw_hbm,
    out, tout,
    mask, arw, rd, sn, tpad, g, gtt, resid, ysend, yrecv, zsend, zru, zrd, pxs, pxr,
    gt, core_in, xs, xr, acc, ys, yr, winf, errf,
    load_sem, send_sem, recv_sem,
):
    blk = lax.axis_index("blk")
    tm = lax.axis_index("tm")
    x, ylo, c = blk // 4, (blk // 2) % 2, blk % 2
    h, z = tm // 8, tm % 8

    def at_blk(x_, ylo_, c_):
        return ((x_ * 2 + ylo_) * 2 + c_, tm)

    up = (blk, h * 8 + (z + 1) % 8)
    down = (blk, h * 8 + (z + 7) % 8)
    pair = (blk, (1 - h) * 8 + z)
    after = (blk, (tm + 1) % 16)
    before = (blk, (tm + 15) % 16)
    other_core = at_blk(x, ylo, 1 - c)
    x_away = [None] + [at_blk((x + d) % 4, ylo, c) for d in (1, 2, 3)]
    y_next = at_blk(x, 1 - ylo, c)
    way = {"u": up, "d": down}

    barrier = pltpu.get_barrier_semaphore()
    partners = [up, down, pair, after, before, other_core, y_next] + x_away[1:]

    t_rows = t_hbm.shape[0]
    t_load = pltpu.make_async_copy(t_hbm, tpad.at[pl.ds(LAG, t_rows)], load_sem.at[16])
    mask_load = pltpu.make_async_copy(mask_hbm, mask, load_sem.at[17])
    arw_load = pltpu.make_async_copy(arw_hbm, arw, load_sem.at[18])

    def owner_of(p):
        d = (p + 1) // 2
        return (z + 8 + 4 + d * (1 - 2 * (p % 2))) % 8

    def half_rows(p, half):
        return pl.multiple_of(owner_of(p) * GROUP + half * HALF, HALF)

    def start_loads(p, half):
        r = half_rows(p, half)
        sem = load_sem.at[2 * p + half]
        pltpu.make_async_copy(sn_hbm.at[pl.ds(r, HALF)], sn.at[pl.ds(r, HALF)], sem).start()
        pltpu.make_async_copy(rd_hbm.at[pl.ds(r, HALF)], rd.at[pl.ds(r, HALF)], sem).start()

    def loaded(p, half):
        both = rd.at[pl.ds(0, HALF + HALF * RANK // t_rows)]
        pltpu.make_async_copy(both, both, load_sem.at[2 * p + half]).wait()

    t_load.start()
    start_loads(0, 0)
    mask_load.start()
    start_loads(0, 1)
    for who in partners:
        pl.semaphore_signal(barrier, inc=1, device_id=who, device_id_type=MESH)

    q_off = [h * TILE, (1 - h) * TILE, (2 + h) * TILE, (3 - h) * TILE]
    q_off = [pl.multiple_of(v, TILE) for v in q_off]

    messages, slots, landed, sent_rows = {}, {}, set(), []

    def define(name, src, dst, who, together=None):
        slot = slots.setdefault(name if together is None else together, len(slots))
        messages[name] = pltpu.make_async_remote_copy(
            src_ref=src, dst_ref=dst, send_sem=send_sem, recv_sem=recv_sem.at[slot],
            device_id=who, device_id_type=MESH,
        )

    def send(name, rows):
        messages[name].start()
        sent_rows.append(rows)

    def need(name):
        if name not in landed:
            landed.add(name)
            messages[name].wait_recv()

    def bytes_of(rows, sem):
        some = rd.at[pl.ds(0, rows * RANK // t_rows)]
        return pltpu.make_async_remote_copy(
            src_ref=some, dst_ref=some, send_sem=send_sem, recv_sem=sem, device_id=pair, device_id_type=MESH
        )

    def need_together(name, rows):
        if name not in landed:
            landed.add(name)
            bytes_of(rows, recv_sem.at[slots[name]]).wait_recv()

    def piece(q, u):
        return pl.ds(pl.multiple_of(q_off[q] + u * PIECE, PIECE), PIECE)

    def out_rows(k, q, u):
        return pl.multiple_of(((z + k) % 8) * GROUP + q_off[q] + u * PIECE, PIECE)

    def compute(p, half):
        loaded(p, half)
        r = half_rows(p, half)
        for j in range(t_rows // COLS):
            cols = slice(j * COLS, (j + 1) * COLS)
            tj = tpad[LAG + j * COLS : LAG + (j + 1) * COLS, :]
            pred = lax.dot_general(
                sn[pl.ds(r, HALF), :], tj, (((1,), (1,)), ((), ())), preferred_element_type=F32
            )
            diff = rd[pl.ds(r, HALF), cols].astype(F32) - pred * (1.0 / math.sqrt(RANK))
            for i in range(HALF // TILE):
                for jj in range(COLS // TILE):
                    tile_row = owner_of(p) * (GROUP // TILE) + half * 2 + i
                    keep = mask[j * (COLS // TILE) + jj, tile_row].astype(F32)
                    block = diff[i * TILE : (i + 1) * TILE, jj * TILE : (jj + 1) * TILE]
                    a, b = half * HALF + i * TILE, j * COLS + jj * TILE
                    resid[a : a + TILE, b : b + TILE] = (block * keep).astype(BF16)
        rows = slice(half * HALF, (half + 1) * HALF)
        g[p, rows, :] = jnp.dot(resid[rows, :], tpad[LAG : LAG + t_rows, :], preferred_element_type=F32)
        if half == 1:
            sensors = sn[pl.ds(half_rows(p, 0), GROUP), :]
            part = lax.dot_general(
                sensors, resid[...], (((0,), (0,)), ((), ())), preferred_element_type=F32
            )
            gtt[...] = part if p == 0 else gtt[...] + part

    def do_a(p):
        compute(p, 0)
        if p == 0:
            for later in range(1, 8):
                start_loads(later, 0)
                start_loads(later, 1)
            arw_load.start()
            pl.semaphore_wait(barrier, len(partners))
            define("rim_up", tpad.at[pl.ds(t_rows, LAG)], tpad.at[pl.ds(0, LAG)], after, "rims")
            define("rim_down", tpad.at[pl.ds(LAG, LAG)], tpad.at[pl.ds(LAG + t_rows, LAG)], before, "rims")

    def do_b(p):
        compute(p, 1)

    def do_y(p, u):
        rows = pl.ds(u * PIECE, PIECE)
        ysend[p, rows, :] = g[p, piece(3, u), :].astype(BF16)
        define(("y", p, u), ysend.at[p, rows], yrecv.at[p, rows], pair)
        send(("y", p, u), PIECE)

    def own(p, q, u):
        part = g[p, piece(q, u), :]
        if q == 2:
            need(("y", p, u))
            part = part + yrecv[p, pl.ds(u * PIECE, PIECE), :].astype(F32)
        return part

    def starts(k, q, d, u):
        longer = {0: "u", 1: "d", 2: "ud"[u * PIECE * 2 // TILE]}[q]
        return k == (4 if d == longer else 3)

    def do_r(k, q, d, u):
        p = PLACE[k] if d == "u" else PLACE[8 - k]
        land = zru if d == "u" else zrd
        rows = pl.ds(q * TILE + u * PIECE, PIECE)
        part = own(p, q, u)
        if not starts(k, q, d, u):
            need(("r", k + 1, q, d, u))
            part = part + land[k, rows, :].astype(F32)
        zsend[p, rows, :] = part.astype(BF16)
        define(("r", k, q, d, u), zsend.at[p, rows], land.at[k - 1, rows], way[d])
        send(("r", k, q, d, u), PIECE)

    def finished(q, u, total):
        r = out_rows(0, q, u)
        sensors = sn[pl.ds(r, PIECE), :].astype(F32)
        out[pl.ds(r, PIECE), :] = (0.9 * sensors + (step_sens / math.sqrt(RANK)) * total).astype(BF16)

    def do_s(q, u):
        rows = pl.ds(q * TILE + u * PIECE, PIECE)
        part = own(7, q, u)
        for d, land in (("u", zru), ("d", zrd)):
            need(("r", 1, q, d, u))
            part = part + land[0, rows, :].astype(F32)
        if q == 0:
            g[7, piece(0, u), :] = part
        elif q == 1:
            here = pl.ds(u * PIECE, PIECE)
            pxs[here, :] = part.astype(BF16)
            define(("s", u), pxs.at[here], pxr.at[here], pair)
            send(("s", u), PIECE)
        else:
            finished(2, u, part)

    def do_f(u):
        need(("s", u))
        finished(0, u, g[7, piece(0, u), :] + pxr[pl.ds(u * PIECE, PIECE), :].astype(F32))
        rows = out.at[pl.ds(out_rows(0, 0, u), PIECE)]
        define(("f", u), rows, rows, pair)
        send(("f", u), PIECE)

    def do_h(s, q, d, u):
        if s > 1:
            need(("h", s - 1, q, d, u))
        elif q == 1:
            need(("f", u))
        k = (9 - s) % 8 if d == "u" else s - 1
        rows = out.at[pl.ds(out_rows(k, q, u), PIECE)]
        last = s == 4 and q < 2 or s == 3 and (q == 0 and d == "d" or q == 1 and d == "u")
        define(("h", s, q, d, u), rows, rows, way[d], "last" if last else None)
        send(("h", s, q, d, u), PIECE)

    def do_x(s, d, u):
        if s > 0:
            need(("h", s, 2, d, u))
        k = (8 - s) % 8 if d == "u" else s
        rows = out.at[pl.ds(out_rows(k, 2, u), PIECE)]
        define(("x", s, d, u), rows, rows, pair, "x")
        send(("x", s, d, u), PIECE)

    half_t = t_rows // 2
    per_x = half_t // 4
    per_y = per_x // 2
    mine = pl.multiple_of(c * half_t, half_t)
    theirs = pl.multiple_of((1 - c) * half_t, half_t)
    x_rows = [pl.multiple_of(((x + d) % 4) * per_x, per_x) for d in range(4)]
    first = pl.multiple_of(mine + x_rows[0] + ylo * per_y, per_y)

    def new_time():
        arw_load.wait()
        need_together("rims", 2 * LAG)
        seen = per_y + 2 * LAG
        win = tpad[pl.ds(first, seen), :].astype(F32)
        step = first - LAG + lax.broadcasted_iota(jnp.int32, (seen, RANK), 0)
        winf[...] = jnp.where((step >= 0) | (tm > 0), win, 0.0)
        errs = per_y + LAG
        err = winf[LAG : LAG + errs, :]
        lags = (1, 12, LAG)
        for i in range(3):
            err = err - arw[i : i + 1, :] * winf[LAG - lags[i] : LAG - lags[i] + errs, :]
        step = first + lax.broadcasted_iota(jnp.int32, (errs, RANK), 0)
        errf[...] = jnp.where((step < t_rows) | (tm < 15), err, 0.0)
        adj = errf[0:per_y, :]
        for i in range(3):
            adj = adj - arw[i : i + 1, :] * errf[lags[i] : lags[i] + per_y, :]
        total = acc[pl.ds(pl.multiple_of(ylo * per_y, per_y), per_y), :] + yr[...].astype(F32)
        new = winf[LAG : LAG + per_y, :] + (step_time / math.sqrt(RANK)) * total - 0.5 * adj
        tout[pl.ds(first, per_y), :] = new.astype(BF16)

    def do_g(n):
        if n == 0:
            send("rim_up", LAG)
            send("rim_down", LAG)
            for j in range(t_rows // COLS):
                gt[j * COLS : (j + 1) * COLS, :] = gtt[:, j * COLS : (j + 1) * COLS].T
            define("core", gt.at[pl.ds(theirs, half_t)], core_in, other_core)
            send("core", 2 * half_t)
        elif n == 1:
            need("core")
            for d in (1, 2, 3):
                rows = x_rows[d]
                total = gt[pl.ds(mine + rows, per_x), :] + core_in[pl.ds(rows, per_x), :]
                xs[d - 1] = total.astype(BF16)
                define(("gx", d), xs.at[d - 1], xr.at[d - 1], x_away[d], "gx")
                send(("gx", d), per_x)
            rows = x_rows[0]
            acc[...] = gt[pl.ds(mine + rows, per_x), :] + core_in[pl.ds(rows, per_x), :]
        elif n == 2:
            need_together("gx", 3 * per_x)
            acc[...] += (xr[0].astype(F32) + xr[1].astype(F32)) + xr[2].astype(F32)
            ys[...] = acc[pl.ds(pl.multiple_of((1 - ylo) * per_y, per_y), per_y), :].astype(BF16)
            define("gy", ys, yr, y_next)
            send("gy", per_y)
        elif n == 3:
            need("gy")
            new_time()
            rows = tout.at[pl.ds(first, per_y)]
            define("ty", rows, rows, y_next)
            send("ty", per_y)
        elif n == 4:
            need("ty")
            rows = tout.at[pl.ds(pl.multiple_of(mine + x_rows[0], per_x), per_x)]
            for d in (1, 2, 3):
                define(("tx", d), rows, rows, x_away[d], "tx")
                send(("tx", d), per_x)
        else:
            need_together("tx", 3 * per_x)
            rows = tout.at[pl.ds(mine, half_t)]
            define("tc", rows, rows, other_core)
            send("tc", half_t)

    t_load.wait()
    mask_load.wait()
    todo = {
        "a": do_a, "b": do_b, "y": do_y, "r": do_r, "s": do_s, "f": do_f, "h": do_h, "x": do_x, "g": do_g
    }
    for step in ORDER:
        todo[step[0]](*(v if v in "ud" else int(v) for v in step[1:]))
    need("tc")
    need_together("x", 8 * TILE)
    need_together("last", 4 * TILE)
    assert all(name in landed for name in slots)
    bytes_of(sum(sent_rows), recv_sem.at[0]).wait_send()


def write_out(new_sensor, new_time, sensor_hbm, time_hbm, sem):
    a = pltpu.make_async_copy(new_sensor, sensor_hbm, sem.at[0])
    b = pltpu.make_async_copy(new_time, time_hbm, sem.at[1])
    a.start()
    b.start()
    a.wait()
    b.wait()


def on_device(readings, tile_mask, sensor_f, time_f, ar_weight):
    sens_here, time_here = readings.shape
    time_total = time_here * lax.axis_size("tm")
    sens_total = sens_here * lax.axis_size("blk")
    rank = sensor_f.shape[1]
    step_sens = 2.0 * math.sqrt(rank / time_total)
    step_time = 2.0 * math.sqrt(rank / sens_total)
    half_t = time_here // 2
    per_x = half_t // 4
    per_y = per_x // 2
    in_vmem = pl.BlockSpec(memory_space=pltpu.VMEM)
    flops = 6 * sens_here * time_here * rank
    operands = (readings, tile_mask.T, sensor_f, time_f, ar_weight)
    new_sensor, new_time = pl.pallas_call(
        functools.partial(kernel, step_sens, step_time),
        out_shape=(
            pltpu.VMEM(sensor_f.shape, BF16),
            pltpu.VMEM(time_f.shape, BF16),
        ),
        in_specs=[pl.BlockSpec(memory_space=pltpu.HBM)] * 5,
        out_specs=(in_vmem, in_vmem),
        scratch_shapes=[
            pltpu.SMEM((time_here // TILE, sens_here // TILE), jnp.int32),
            pltpu.VMEM((3, rank), F32),
            pltpu.VMEM((sens_here, time_here), BF16),
            pltpu.VMEM((sens_here, rank), BF16),
            pltpu.VMEM((time_here + 2 * LAG, rank), BF16),
            pltpu.VMEM((8, GROUP, rank), F32),
            pltpu.VMEM((rank, time_here), F32),
            pltpu.VMEM((GROUP, time_here), BF16),
            pltpu.VMEM((8, TILE, rank), BF16),
            pltpu.VMEM((8, TILE, rank), BF16),
            pltpu.VMEM((8, 3 * TILE, rank), BF16),
            pltpu.VMEM((4, 3 * TILE, rank), BF16),
            pltpu.VMEM((4, 3 * TILE, rank), BF16),
            pltpu.VMEM((TILE, rank), BF16),
            pltpu.VMEM((TILE, rank), BF16),
            pltpu.VMEM((time_here, rank), F32),
            pltpu.VMEM((half_t, rank), F32),
            pltpu.VMEM((3, per_x, rank), BF16),
            pltpu.VMEM((3, per_x, rank), BF16),
            pltpu.VMEM((per_x, rank), F32),
            pltpu.VMEM((per_y, rank), BF16),
            pltpu.VMEM((per_y, rank), BF16),
            pltpu.VMEM((per_y + 2 * LAG, rank), F32),
            pltpu.VMEM((per_y + LAG, rank), F32),
            pltpu.SemaphoreType.DMA((19,)),
            pltpu.SemaphoreType.DMA,
            pltpu.SemaphoreType.DMA((MESSAGES,)),
        ],
        compiler_params=pltpu.CompilerParams(
            collective_id=0, has_side_effects=True, vmem_limit_bytes=48 * 1024 * 1024
        ),
        cost_estimate=pl.CostEstimate(
            flops=flops, bytes_accessed=2 * sens_here * time_here, transcendentals=0
        ),
        name="sweep",
    )(*[pltpu.with_memory_space_constraint(v, pltpu.HBM) for v in operands])
    in_hbm = pl.BlockSpec(memory_space=pltpu.HBM)
    return pl.pallas_call(
        write_out,
        out_shape=(pltpu.HBM(sensor_f.shape, BF16), pltpu.HBM(time_f.shape, BF16)),
        in_specs=[in_vmem, in_vmem],
        out_specs=(in_hbm, in_hbm),
        scratch_shapes=[pltpu.SemaphoreType.DMA((2,))],
        name="write_out",
    )(*[pltpu.with_memory_space_constraint(v, pltpu.VMEM) for v in (new_sensor, new_time)])


def solution(mesh):
    return jax.shard_map(
        on_device,
        mesh=mesh,
        in_specs=(P("blk", "tm"), P("blk", "tm"), P("blk", None), P("tm", None), P()),
        out_specs=(P("blk", None), P("tm", None)),
        check_vma=False,
    )
```

time: 350 us -> 51.7 us (0.15)
  waiting for transfers between devices: 287 us -> 0 us
  Pallas kernels: 0 us -> 51 us
  matrix products: 22.6 us -> 0 us
  between operations: 14.1 us -> 0.64 us
  local copies, waits for them, and re-layouts: 11.2 us -> 0 us
  other arithmetic: 9.51 us -> 0 us
  starting transfers between devices: 5.18 us -> 0 us
    psum x2 -> x0, waiting for transfers between devices: 280 us -> none  [the longest x1 179 us: on_device(): lax.psum(jnp.dot(resid, time_f, preferred_element_type=jnp.float32) * sca...]
    pallas_call x0 -> x2, Pallas kernels: none -> 51 us  [the longest x1 49.5 us: on_device(): pl.pallas_call(functools.partial(kernel, step_sens, step_time), out_shape...]
    dot_general x3 -> x0, matrix products: 22.6 us -> none  [the longest x1 11.6 us: on_device(): jnp.dot(sensor_f, time_f.T, preferred_element_type=jnp.float32) * scale]
    convert_element_type x5 -> x0, other arithmetic: 9.16 us -> none  [the longest x1 4.26 us: on_device(): (factor + step_time * grad_t - 0.5 * ar_adj).astype(jnp.bfloat16)]
    mul x1 -> x0, local copies, waits for them, and re-layouts: 6.88 us -> none  [on_device(): resid = (diff * keep).reshape(sens_here, time_here).astype(jnp.bfloat16)]
    ppermute x2 -> x0, waiting for transfers between devices: 6.72 us -> none  [passed_along(): return lax.ppermute(block, axis, route)]
    ppermute x2 -> x0, starting transfers between devices: 5.1 us -> none  [passed_along(): return lax.ppermute(block, axis, route)]
    unnamed x10 -> x0, local copies, waits for them, and re-layouts: 4.2 us -> none
  transfers between devices with their start and end apart: 4 -> 0, of which waited for: 4 -> 0; matrix products, arithmetic and copies ran while one was open for 4% -> 0% of each run, Pallas kernels for 0% -> 0%
where the time goes in v3:
time: 51.7 us; the launch traced here: 51.6 us
  Pallas kernels  51 us (99%)
  between operations  0.64 us (1%)
    pallas_call x1, Pallas kernels, on_device(): pl.pallas_call(functools.partial(kernel, step_sens, step_time), out_shape...  49.5 us
    pallas_call x1, Pallas kernels, on_device(): pl.pallas_call(write_out, out_shape=(pltpu.HBM(sensor_f.shape, BF16), plt...  1.5 us

profile of v3, /device:TPU:2, one launch (start us, length us, event | category | flops | bytes accessed | tf_op | source)
XLA Modules:
  0.0 51.6 jit_solution(17107070489388720095)
XLA Ops:
  0.6 49.5 %sweep.1 = (bf16[4096,256]{1,0:T(8,128)(2,1)S(1)}, bf16[1024,256]{1,0:T(8,128)(2,1)S(1)}) custom-call(bf16[4096,1024]{1,0:T(8,128)(2,1)} %rd_hbm.1, s32[8,32]{1,0:T(8,128)} %bitcast.1, bf16[4096,256]{1,0:T(8,128)(2,1)} %sn_hbm.1, bf16[1024,256]{1,0:T(8,128)(2,1)} %t_hbm.1, f32[3,256]{1,0:T(4,128)} %arw_hbm.1), custom_call_target="tpu_custom_call" | custom-call | flops 6442450944 | bytes 8388608 | tf_op jit(solution)/shard_map/sweep/pallas_call | solution.py:360
  50.1 1.5 %write_out.1 = (bf16[4096,256]{1,0:T(8,128)(2,1)}, bf16[1024,256]{1,0:T(8,128)(2,1)}) custom-call(bf16[4096,256]{1,0:T(8,128)(2,1)S(1)} %get-tuple-element.4.new_sensor, bf16[1024,256]{1,0:T(8,128)(2,1)S(1)} %get-tuple-element.5.new_time), custom_call_target="tpu_custom_call" | custom-call | tf_op jit(solution)/shard_map/write_out/pallas_call | solution.py:406

commit v4 on v3

--- a/solution.py
+++ b/solution.py
@@ -15,7 +15,8 @@
 HALF = 2 * TILE
 PIECE = TILE // 2
 COLS = 256
-MESSAGES = 105
+Y_PIECES = 2
+MESSAGES = 98
 MESH = pl.DeviceIdType.MESH
 F32 = jnp.float32
 BF16 = jnp.bfloat16
@@ -24,11 +25,11 @@
 
 ORDER = (
     "a0", "r41d0", "b0", "y01", "r40u1", "a1", "r41d1", "y00", "r40u0", "b1", "a2", "r30d0", "r31u0", "y11",
-    "r31u1", "b2", "r30d1", "y21", "y20", "a3", "r31d0", "r30u1", "b3", "r42d1", "r30u0", "r31d1", "y10",
-    "r42u0", "a4", "y31", "r21u0", "b4", "r32u1", "r20d0", "y41", "a5", "r21u1", "y30", "r21d0", "b5",
-    "r32d1", "r20u1", "a6", "r21d1", "r32d0", "y40", "r32u0", "b6", "r20d1", "y61", "r20u0", "y51", "r11u0",
-    "a7", "y50", "y60", "r11d0", "r22u1", "b7", "r22d1", "r11u1", "r11d1", "g0", "r22u0", "r22d0", "r10d0",
-    "y71", "r10u0", "s10", "y70", "r12u1", "r12d1", "r10u1", "r10d1", "g1", "s11", "r12u0", "r12d0", "s00",
+    "r31u1", "b2", "r30d1", "y21", "a3", "r31d0", "r30u1", "b3", "r42d1", "r30u0", "r31d1",
+    "r42u0", "a4", "y31", "r21u0", "b4", "r32u1", "r20d0", "y41", "a5", "r21u1", "r21d0", "b5",
+    "r32d1", "r20u1", "a6", "r21d1", "r32d0", "r32u0", "b6", "r20d1", "y61", "r20u0", "y51", "r11u0",
+    "a7", "r11d0", "r22u1", "b7", "r22d1", "r11u1", "r11d1", "g0", "r22u0", "r22d0", "r10d0",
+    "y71", "r10u0", "s10", "r12u1", "r12d1", "r10u1", "r10d1", "g1", "s11", "r12u0", "r12d0", "s00",
     "f0", "s21", "h12d1", "h12u1", "x0u1", "h10u0", "h10d0", "s01", "s20", "h12d0", "h12u0", "f1", "h10d1",
     "x0u0", "h10u1", "x1d1", "h22u1", "h22d1", "g2", "h11u0", "h11d0", "h22u0", "h22d0", "x1d0", "x1u1",
     "h20u1", "h11d1", "h20d1", "h11u1", "h32d1", "h32u1", "x2d1", "g3", "x2u1", "h21d0", "h32u0", "h20u0",
@@ -101,21 +102,18 @@
 
     messages, slots, landed, sent_rows = {}, {}, set(), []
 
+    def arrival(name):
+        return recv_sem.at[slots.setdefault(name, len(slots))]
+
     def define(name, src, dst, who, together=None):
-        slot = slots.setdefault(name if together is None else together, len(slots))
         messages[name] = pltpu.make_async_remote_copy(
-            src_ref=src, dst_ref=dst, send_sem=send_sem, recv_sem=recv_sem.at[slot],
+            src_ref=src, dst_ref=dst, send_sem=send_sem, recv_sem=arrival(name if together is None else together),
             device_id=who, device_id_type=MESH,
         )
 
     def send(name, rows):
         messages[name].start()
         sent_rows.append(rows)
-
-    def need(name):
-        if name not in landed:
-            landed.add(name)
-            messages[name].wait_recv()
 
     def bytes_of(rows, sem):
         some = rd.at[pl.ds(0, rows * RANK // t_rows)]
@@ -123,10 +121,10 @@
             src_ref=some, dst_ref=some, send_sem=send_sem, recv_sem=sem, device_id=pair, device_id_type=MESH
         )
 
-    def need_together(name, rows):
+    def need(name, rows=PIECE):
         if name not in landed:
             landed.add(name)
-            bytes_of(rows, recv_sem.at[slots[name]]).wait_recv()
+            bytes_of(rows, arrival(name)).wait_recv()
 
     def piece(q, u):
         return pl.ds(pl.multiple_of(q_off[q] + u * PIECE, PIECE), PIECE)
@@ -158,32 +156,31 @@
             part = lax.dot_general(
                 sensors, resid[...], (((0,), (0,)), ((), ())), preferred_element_type=F32
             )
-            gtt[...] = part if p == 0 else gtt[...] + part
-
-    def do_a(p):
-        compute(p, 0)
-        if p == 0:
-            for later in range(1, 8):
-                start_loads(later, 0)
-                start_loads(later, 1)
-            arw_load.start()
-            pl.semaphore_wait(barrier, len(partners))
-            define("rim_up", tpad.at[pl.ds(t_rows, LAG)], tpad.at[pl.ds(0, LAG)], after, "rims")
-            define("rim_down", tpad.at[pl.ds(LAG, LAG)], tpad.at[pl.ds(LAG + t_rows, LAG)], before, "rims")
-
-    def do_b(p):
-        compute(p, 1)
+            gtt[...] += part
+
+    def begin():
+        for later in range(1, 8):
+            start_loads(later, 0)
+            start_loads(later, 1)
+        arw_load.start()
+        pl.semaphore_wait(barrier, len(partners))
 
     def do_y(p, u):
-        rows = pl.ds(u * PIECE, PIECE)
-        ysend[p, rows, :] = g[p, piece(3, u), :].astype(BF16)
+        u = u if p == 0 else 0
+        size = TILE // Y_PIECES if p == 0 else TILE
+        rows = pl.ds(u * size, size)
+        part = g[p, pl.ds(pl.multiple_of(q_off[3] + u * size, size), size), :]
+        ysend[p, rows, :] = part.astype(BF16)
         define(("y", p, u), ysend.at[p, rows], yrecv.at[p, rows], pair)
-        send(("y", p, u), PIECE)
+        send(("y", p, u), size)
 
     def own(p, q, u):
         part = g[p, piece(q, u), :]
         if q == 2:
-            need(("y", p, u))
+            if p == 0:
+                need(("y", p, u * PIECE * Y_PIECES // TILE), TILE // Y_PIECES)
+            elif u == 1:
+                need(("y", p, 0), TILE)
             part = part + yrecv[p, pl.ds(u * PIECE, PIECE), :].astype(F32)
         return part
 
@@ -260,7 +257,7 @@
 
     def new_time():
         arw_load.wait()
-        need_together("rims", 2 * LAG)
+        need("rims", 2 * LAG)
         seen = per_y + 2 * LAG
         win = tpad[pl.ds(first, seen), :].astype(F32)
         step = first - LAG + lax.broadcasted_iota(jnp.int32, (seen, RANK), 0)
@@ -281,6 +278,8 @@
 
     def do_g(n):
         if n == 0:
+            define("rim_up", tpad.at[pl.ds(t_rows, LAG)], tpad.at[pl.ds(0, LAG)], after, "rims")
+            define("rim_down", tpad.at[pl.ds(LAG, LAG)], tpad.at[pl.ds(LAG + t_rows, LAG)], before, "rims")
             send("rim_up", LAG)
             send("rim_down", LAG)
             for j in range(t_rows // COLS):
@@ -288,7 +287,7 @@
             define("core", gt.at[pl.ds(theirs, half_t)], core_in, other_core)
             send("core", 2 * half_t)
         elif n == 1:
-            need("core")
+            need("core", 2 * half_t)
             for d in (1, 2, 3):
                 rows = x_rows[d]
                 total = gt[pl.ds(mine + rows, per_x), :] + core_in[pl.ds(rows, per_x), :]
@@ -298,39 +297,71 @@
             rows = x_rows[0]
             acc[...] = gt[pl.ds(mine + rows, per_x), :] + core_in[pl.ds(rows, per_x), :]
         elif n == 2:
-            need_together("gx", 3 * per_x)
+            need("gx", 3 * per_x)
             acc[...] += (xr[0].astype(F32) + xr[1].astype(F32)) + xr[2].astype(F32)
             ys[...] = acc[pl.ds(pl.multiple_of((1 - ylo) * per_y, per_y), per_y), :].astype(BF16)
             define("gy", ys, yr, y_next)
             send("gy", per_y)
         elif n == 3:
-            need("gy")
+            need("gy", per_y)
             new_time()
             rows = tout.at[pl.ds(first, per_y)]
             define("ty", rows, rows, y_next)
             send("ty", per_y)
         elif n == 4:
-            need("ty")
+            need("ty", per_y)
             rows = tout.at[pl.ds(pl.multiple_of(mine + x_rows[0], per_x), per_x)]
             for d in (1, 2, 3):
                 define(("tx", d), rows, rows, x_away[d], "tx")
                 send(("tx", d), per_x)
         else:
-            need_together("tx", 3 * per_x)
+            need("tx", 3 * per_x)
             rows = tout.at[pl.ds(mine, half_t)]
             define("tc", rows, rows, other_core)
             send("tc", half_t)
 
+    todo = {"y": do_y, "r": do_r, "s": do_s, "f": do_f, "h": do_h, "x": do_x, "g": do_g}
+
+    def run(steps):
+        for step in steps:
+            if step == "a0":
+                begin()
+            elif step[0] not in "ab":
+                todo[step[0]](*(v if v in "ud" else int(v) for v in step[1:]))
+
+    def run_one(p, low, parts):
+        if len(parts) == 1:
+            run(parts[0])
+        else:
+            middle = len(parts) // 2
+
+            @pl.when(p < low + middle)
+            def _():
+                run_one(p, low, parts[:middle])
+
+            @pl.when(p >= low + middle)
+            def _():
+                run_one(p, low + middle, parts[middle:])
+
+    starts_at = [ORDER.index(half + str(p)) for p in range(8) for half in "ab"]
+    parts = [ORDER[i:j] for i, j in zip(starts_at, starts_at[1:] + [len(ORDER)])]
+    parts, rest = parts[:15] + [()], parts[15]
+    gtt[...] = jnp.zeros_like(gtt)
     t_load.wait()
     mask_load.wait()
-    todo = {
-        "a": do_a, "b": do_b, "y": do_y, "r": do_r, "s": do_s, "f": do_f, "h": do_h, "x": do_x, "g": do_g
-    }
-    for step in ORDER:
-        todo[step[0]](*(v if v in "ud" else int(v) for v in step[1:]))
-    need("tc")
-    need_together("x", 8 * TILE)
-    need_together("last", 4 * TILE)
+
+    def group(p, carry):
+        compute(p, 0)
+        run_one(p, 0, parts[0::2])
+        compute(p, 1)
+        run_one(p, 0, parts[1::2])
+        return carry
+
+    lax.fori_loop(0, 8, group, 0)
+    run(rest)
+    need("tc", half_t)
+    need("x", 8 * TILE)
+    need("last", 4 * TILE)
     assert all(name in landed for name in slots)
     bytes_of(sum(sent_rows), recv_sem.at[0]).wait_send()
 

time: 51.7 us -> 52.2 us (level)
  no operation moved by 1% of the time
where the time goes in v4:
time: 52.2 us; the launch traced here: 52.1 us
  Pallas kernels  51.4 us (98%)
  between operations  0.64 us (1%)
    pallas_call x1, Pallas kernels, on_device(): pl.pallas_call(functools.partial(kernel, step_sens, step_time), out_shape...  49.9 us
    pallas_call x1, Pallas kernels, on_device(): pl.pallas_call(write_out, out_shape=(pltpu.HBM(sensor_f.shape, BF16), plt...  1.5 us

profile of v4, /device:TPU:2, one launch (start us, length us, event | category | flops | bytes accessed | tf_op | source)
XLA Modules:
  0.0 52.1 jit_solution(9069845536769347778)
XLA Ops:
  0.6 49.9 %sweep.1 = (bf16[4096,256]{1,0:T(8,128)(2,1)S(1)}, bf16[1024,256]{1,0:T(8,128)(2,1)S(1)}) custom-call(bf16[4096,1024]{1,0:T(8,128)(2,1)} %rd_hbm.1, s32[8,32]{1,0:T(8,128)} %bitcast.1, bf16[4096,256]{1,0:T(8,128)(2,1)} %sn_hbm.1, bf16[1024,256]{1,0:T(8,128)(2,1)} %t_hbm.1, f32[3,256]{1,0:T(4,128)} %arw_hbm.1), custom_call_target="tpu_custom_call" | custom-call | flops 6442450944 | bytes 8388608 | tf_op jit(solution)/shard_map/sweep/pallas_call | solution.py:391
  50.5 1.5 %write_out.1 = (bf16[4096,256]{1,0:T(8,128)(2,1)}, bf16[1024,256]{1,0:T(8,128)(2,1)}) custom-call(bf16[4096,256]{1,0:T(8,128)(2,1)S(1)} %get-tuple-element.4.new_sensor, bf16[1024,256]{1,0:T(8,128)(2,1)S(1)} %get-tuple-element.5.new_time), custom_call_target="tpu_custom_call" | custom-call | tf_op jit(solution)/shard_map/write_out/pallas_call | solution.py:437
